TPU v7x, 512 devices: a whole 4x4x16 slice. The times are simulated.
512 devices in a mesh: row: 16 (over z), col: 32 (over x, y, core).
Axes of the slice: x: 4, y: 4, z: 16, core: 2. Of those that a mesh axis runs over, the one named last changes fastest.
Arguments:
- features: bfloat16 [65536, 128], P(('row', 'col')), may hold values from -6 to 6
- weight: bfloat16 [128, 256], replicated, may hold values from -0.5 to 0.5
- bias: float32 [256], replicated, may hold values from -3 to 3
- adj_values: bfloat16 [16, 512, 6, 128, 128], P('row', 'col'), may hold values from -0.109375 to 0.109375
- adj_rows: int32 [16, 512, 6], P('row', 'col'), may hold values from -1 to 31, as said below
- cotangent: bfloat16 [65536, 256], P(('row', 'col')), may hold values from -6 to 6
Outputs:
- activations: bfloat16 [65536, 256], P(('row', 'col'))
- dfeatures: bfloat16 [65536, 128], P(('row', 'col'))
- dweight: float32 [128, 256], replicated
- dbias: float32 [256], replicated
Inputs may be any that keep to these rules, and one draw needn't show every extreme that they name: `adj_rows`: in each block column of each tile the live slots come first and name distinct block rows, the rest are -1; every tile has some block column with all 6 slots live.
All inputs are finite; a program needn't handle non-finite values.
Results may differ from a plain program's by a relative error of at most 0.024.
Values may be sent and summed in bfloat16 or wider, within the bound.
A program may use at most 128 MiB of HBM per device.

v0:
```python
import jax
import jax.numpy as jnp
from jax import lax
from jax.sharding import PartitionSpec as P

F_OUT = 256
BLOCK = 128
SLOTS = 6


def local(features, weight, bias, adj_values, adj_rows, cotangent):
    node_rows = features.shape[0]
    row_blocks = lax.axis_size("col") * (node_rows // BLOCK)
    blocks = adj_values[0]
    col_blocks = blocks.shape[0]
    slot_ids = adj_rows[0].reshape(col_blocks * SLOTS)
    live_ids = jnp.where(slot_ids >= 0, slot_ids, row_blocks)
    transformed = jnp.dot(features, weight, preferred_element_type=jnp.float32).astype(jnp.bfloat16)
    column_list = lax.all_gather(transformed, "row", axis=0, tiled=True)
    block_count_total = blocks.shape[0]
    contrib = jnp.einsum(
        "tsij,tjf->tsif",
        blocks,
        column_list.reshape(block_count_total, BLOCK, F_OUT),
        preferred_element_type=jnp.float32,
    )
    products = contrib.reshape(block_count_total * SLOTS, BLOCK * F_OUT)
    shifted = live_ids - 0
    inside = (shifted >= 0) & (shifted < row_blocks)
    local_ids = jnp.where(inside, shifted, row_blocks)
    placed = jax.ops.segment_sum(products, local_ids, num_segments=row_blocks)
    hidden = lax.psum_scatter(
        placed.reshape(row_blocks * BLOCK, F_OUT).astype(jnp.bfloat16),
        "col",
        scatter_dimension=0,
        tiled=True,
    ).astype(jnp.float32)
    preact = hidden + bias[None, :]
    gate = jax.nn.sigmoid(preact)
    activations = (preact * gate).astype(jnp.bfloat16)
    dpre = cotangent.astype(jnp.float32) * gate * (1.0 + preact * (1.0 - gate))
    grad_rows = lax.all_gather(dpre.astype(jnp.bfloat16), "col", axis=0, tiled=True)
    bias_local = jnp.sum(dpre, axis=0)
    grad_flat = grad_rows.reshape(row_blocks, BLOCK * F_OUT)
    block_count_total = node_rows * lax.axis_size("row") // BLOCK
    picked = jnp.take(grad_flat, live_ids, axis=0, mode="fill", fill_value=0)
    picked = picked.reshape(block_count_total, SLOTS, BLOCK, F_OUT)
    contrib = jnp.einsum("tsij,tsif->tjf", blocks, picked, preferred_element_type=jnp.float32)
    dtransformed = lax.psum_scatter(
        contrib.reshape(block_count_total * BLOCK, F_OUT).astype(jnp.bfloat16),
        "row",
        scatter_dimension=0,
        tiled=True,
    )
    dfeatures = jnp.dot(dtransformed, weight.T, preferred_element_type=jnp.float32).astype(
        jnp.bfloat16
    )
    weight_local = jnp.dot(features.T, dtransformed, preferred_element_type=jnp.float32)
    dweight, dbias = lax.psum((weight_local, bias_local), ("row", "col"))
    return (activations, dfeatures, dweight, dbias)


def solution(mesh):
    return jax.shard_map(
        local,
        mesh=mesh,
        in_specs=(
            P(("row", "col"), None),
            P(),
            P(),
            P("row", "col", None, None, None),
            P("row", "col", None),
            P(("row", "col"), None),
        ),
        out_specs=(P(("row", "col"), None), P(("row", "col"), None), P(), P()),
        check_vma=False,
    )
```

profile of v0, /device:TPU:1, one launch (start us, length us, event | category | flops | bytes accessed | tf_op | source)
XLA Modules:
  0.0 880.6 jit_solution(6773198029193806574)
XLA Ops:
  7.2 0.0 copy-start
  7.2 0.0 all-gather.3.cloned.1.call-start
  7.2 1.8 convolution_convert_fusion
  9.0 0.0 all-gather.3.cloned.1.call-update
  9.0 0.0 reduce-scatter.3.cloned.1.call-start
  9.1 0.8 copy.15
  9.9 0.1 reshape_squeeze.5
  10.0 67.6 %all-gather.3.cloned.1.call-done = bf16[2048,256]{1,0:T(8,128)(2,1)} async-done(((bf16[128,256]{1,0:T(8,128)(2,1)}), bf16[2048,256]{1,0:T(8,128)(2,1)}) %all-gather.3.cloned.1.call-update) | async-done | bytes 1048592 | tf_op jit(solution)/shard_map/all_gather | solution.py:19
  77.6 0.0 copy-done
  77.6 7.6 convolution_bitcast_fusion
  85.2 12.7 %copy.27 = f32[12,8,128,256]{3,1,2,0:T(8,128)} copy(f32[12,8,128,256]{2,3,1,0:T(8,128)} %bitcast.44) | data formatting | bytes 25165824
  97.9 20.5 %scatter_custom_fusion = f32[32,32768]{1,0:T(8,128)} fusion(s32[96]{0:T(128)S(1)} %get-tuple-element.16, f32[96,32768]{1,0:T(8,128)} %bitcast.46, f32[]{:T(128)} %constant.6.clone.1), kind=kCustom, calls=%fused_computation.10 | custom fusion | flops 3145728 | bytes 4194816 | tf_op jit(solution)/shard_map/scatter-add | solution.py:31
  118.3 3.7 convert_element_type.34
  122.0 0.0 copy-start.3
  122.0 0.0 copy-start.5
  122.0 0.0 copy-start.4
  122.0 4.2 convert_element_type.35
  126.3 0.0 reduce-scatter.3.cloned.1.call-update
  126.3 0.0 all-gather.5.cloned.1.call-start
  126.3 106.7 %reduce-scatter.3.cloned.1.call-done = bf16[128,256]{1,0:T(8,128)(2,1)} async-done(((bf16[4096,256]{1,0:T(8,128)(2,1)}), bf16[128,256]{1,0:T(8,128)(2,1)}) %reduce-scatter.3.cloned.1.call-update) | async-done | bytes 65552 | tf_op jit(solution)/shard_map/reduce_scatter | solution.py:32
  233.0 0.0 copy-done.3
  233.1 0.0 copy-done.5
  233.1 1.6 fusion.15
  234.6 0.0 all-gather.5.cloned.1.call-update
  234.6 0.0 reduce-scatter.5.cloned.1.call-start
  234.7 0.0 copy-done.4
  234.7 0.1 copy.18
  234.8 62.6 %all-gather.5.cloned.1.call-done = bf16[4096,256]{1,0:T(8,128)(2,1)} async-done(((bf16[128,256]{1,0:T(8,128)(2,1)}), bf16[4096,256]{1,0:T(8,128)(2,1)}) %all-gather.5.cloned.1.call-update) | async-done | bytes 2097168 | tf_op jit(solution)/shard_map/all_gather | solution.py:42
  297.5 4.2 reshape.84
  301.7 14.4 %gather_fusion = bf16[96,32768]{1,0:T(8,128)(2,1)} fusion(bf16[32,32768]{1,0:T(8,128)(2,1)} %reshape.84, s32[1024]{0:T(1024)S(1)} %pad_clamp_fusion), kind=kCustom, calls=%fused_computation | custom fusion | bytes 12583296 | tf_op jit(solution)/shard_map/jit(_take)/gather | solution.py:46
  316.1 4.7 copy.28
  320.8 0.0 copy-start.2
  320.8 0.0 copy-start.1
  320.8 2.5 bitcast_convert_fusion
  323.3 0.0 reduce-scatter.5.cloned.1.call-update
  323.3 0.0 all-reduce.2.cloned.1.call-start
  323.4 103.8 %psum.15 = f32[256]{0:T(256)} all-reduce(f32[256]{0:T(256)S(1)} %get-tuple-element.12), channel_id=1, replica_groups=mesh['row'=16,'col'=32] {'row','col'}, use_global_device_ids=true, to_apply=%region_5.6 | all-reduce | flops 256 | bytes 2048 | tf_op jit(solution)/shard_map/psum | solution.py:59
  427.2 0.0 reduce-scatter.5.cloned.1.call-done
  427.2 0.0 copy-done.2
  427.2 1.7 convolution_bitcast_fusion.1
  428.9 0.0 all-reduce.2.cloned.1.call-update
  428.9 0.0 copy-done.1
  428.9 1.6 convolution_convert_fusion.1
  430.5 441.9 %all-reduce.2.cloned.1.call-done = f32[128,256]{0,1:T(8,128)} async-done(((f32[128,256]{0,1:T(8,128)}), f32[128,256]{0,1:T(8,128)}) %all-reduce.2.cloned.1.call-update) | async-done | bytes 131088 | tf_op jit(solution)/shard_map/psum | solution.py:59
  872.4 1.7 copy.20
  (3 shorter events, 0.0 us)
Async XLA Ops:
  7.2 70.4 %copy-start = (bf16[1,16,6,128,128]{4,3,2,1,0:T(8,128)(2,1)S(1)}, bf16[1,16,6,128,128]{4,3,2,1,0:T(8,128)(2,1)}, u32[]{:S(2)}) copy-start(bf16[1,16,6,128,128]{4,3,2,1,0:T(8,128)(2,1)} %param.9) | copy-start | bytes 9437188
  7.2 70.4 %all-gather.3.cloned.1.call-start = ((), (), s32[]{:S(2)}) async-start(), calls=%async_computation.2 | async-start | bytes 1114112 | tf_op jit(solution)/shard_map/all_gather | solution.py:19
  9.0 224.0 %reduce-scatter.3.cloned.1.call-start = ((), (), s32[]{:S(2)}) async-start(), calls=%async_computation.3 | async-start | bytes 2162688 | tf_op jit(solution)/shard_map/reduce_scatter | solution.py:32
  122.0 111.0 %copy-start.3 = (bf16[128,256]{1,0:T(8,128)(2,1)S(1)}, bf16[128,256]{1,0:T(8,128)(2,1)}, u32[]{:S(2)}) copy-start(bf16[128,256]{1,0:T(8,128)(2,1)} %param.11) | copy-start | bytes 196612
  122.0 111.0 %copy-start.5 = (f32[256]{0:T(256)S(1)}, f32[256]{0:T(256)}, u32[]{:S(2)}) copy-start(f32[256]{0:T(256)} %param.8) | copy-start | bytes 3076
  122.0 112.7 %copy-start.4 = (s32[1,16,6]{1,0,2:T(1,128)S(1)}, s32[1,16,6]{1,0,2:T(1,128)}, u32[]{:S(2)}) copy-start(s32[1,16,6]{1,0,2:T(1,128)} %param.10) | copy-start | bytes 1156
  126.3 171.2 %all-gather.5.cloned.1.call-start = ((), (), s32[]{:S(2)}) async-start(), calls=%async_computation.4 | async-start | bytes 2162688 | tf_op jit(solution)/shard_map/all_gather | solution.py:42
  234.6 192.5 %reduce-scatter.5.cloned.1.call-start = ((), (), s32[]{:S(2)}) async-start(), calls=%async_computation.5 | async-start | bytes 1114112 | tf_op jit(solution)/shard_map/reduce_scatter | solution.py:49
  320.8 106.4 %copy-start.2 = (bf16[128,128]{1,0:T(8,128)(2,1)S(1)}, bf16[128,128]{1,0:T(8,128)(2,1)}, u32[]{:S(2)}) copy-start(bf16[128,128]{1,0:T(8,128)(2,1)} %param.6) | copy-start | bytes 98308
  320.8 108.1 %copy-start.1 = (bf16[128,256]{1,0:T(8,128)(2,1)S(1)}, bf16[128,256]{1,0:T(8,128)(2,1)}, u32[]{:S(2)}) copy-start(bf16[128,256]{1,0:T(8,128)(2,1)} %param.7) | copy-start | bytes 196612
  323.3 549.1 %all-reduce.2.cloned.1.call-start = ((), (), s32[]{:S(2)}) async-start(), calls=%async_computation.6 | async-start | bytes 262144 | tf_op jit(solution)/shard_map/psum | solution.py:59
Sparse Core Ops, SparseCore 0:
  10.7 66.8 all-gather.2
  126.4 106.6 reduce-scatter.2
  236.8 60.6 all-gather.4
  323.5 59.5 reduce-scatter.4
  429.0 443.3 all-reduce.1
where the time goes:
time: 881 us
  waiting for transfers between devices  679 us (77%)
  blocking collectives  104 us (12%)
  local copies, waits for them, and re-layouts  42.8 us (5%)
  other arithmetic  25.8 us (3%)
  matrix products  15.2 us (2%)
  between operations  13.9 us (2%)
    psum x1, waiting for transfers between devices, local(): dweight, dbias = lax.psum((weight_local, bias_local), ('row', 'col'))  442 us
    reduce_scatter x1, waiting for transfers between devices, local(): lax.psum_scatter(placed.reshape(row_blocks * BLOCK, F_OUT).astype(jnp.bfl...  107 us
    psum x1, blocking collectives, local(): dweight, dbias = lax.psum((weight_local, bias_local), ('row', 'col'))  104 us
    all_gather x1, waiting for transfers between devices, local(): column_list = lax.all_gather(transformed, 'row', axis=0, tiled=True)  67.6 us
    all_gather x1, waiting for transfers between devices, local(): lax.all_gather(dpre.astype(jnp.bfloat16), 'col', axis=0, tiled=True)  62.6 us
    scatter-add x1, other arithmetic, local(): placed = jax.ops.segment_sum(products, local_ids, num_segments=row_blocks)  20.5 us
    unnamed x16, local copies, waits for them, and re-layouts  19.8 us
  transfers between devices with their start and end apart: 5, of which 4 were waited for; matrix products, arithmetic and copies ran while one was open for 0% of the time, Pallas kernels for 0%

commit v1 on v0

v1 whole, which is shorter than its diff:
```python
import jax
import jax.numpy as jnp
from jax import lax
from jax.experimental import pallas as pl
from jax.experimental.pallas import tpu as pltpu
from jax.sharding import PartitionSpec as P

MESH = pl.DeviceIdType.MESH
BF16 = jnp.bfloat16
F32 = jnp.float32
BLOCK = 128
F_IN = 128
F_OUT = 256
SLOTS = 6
NZ = 16
SIDE = 4
CHIPS = SIDE * SIDE
NCOL = 2 * CHIPS
DEAD = NZ * SLOTS
FAR_FIRST = (8, 7, -7, -6, 6, 5, -5, -4, 4, 3, -3, -2, 2, 1, -1)


def remote(src, dst, send_sem, recv_sem, device):
    return pltpu.make_async_remote_copy(
        src_ref=src,
        dst_ref=dst,
        send_sem=send_sem,
        recv_sem=recv_sem,
        device_id=device,
        device_id_type=MESH,
    )


def toward(b):
    if abs(b) <= 2:
        return 0
    return b - 2 if b > 0 else b + 2


def behind(b):
    far = b + 2 if b > 0 else b - 2
    return far if far in FAR_FIRST else None


def kernel(
    adj, feat, weight, bias, vals, cot,
    act_out, df_out, dw_out, db_out,
    xa, blk, prod, inv, w_v, b_v, c_v, act_v,
    sd, rd, sz, rz, ga, own, sb, rb, df_v,
    dwp, dwr, dwm, dwx, dwz, dwf, dwo, dbo,
    lsem, zs, zr, ds, dr, xs, xr, gs, gr, fs, fr, bs, br, ws, wr,
    wxs, wxr, wzs, wzr, was, war,
):
    z = lax.axis_index("row")
    c = lax.axis_index("col")
    px, py, core = c // 8, (c // 2) % 4, c % 2
    other = 1 - core

    def ring(off):
        return lax.rem(z + (off + 2 * NZ), NZ)

    def at_z(off):
        return (ring(off), c)

    def chip(i, sign):
        j = lax.rem(i + 1, CHIPS)
        dx, dy = j // SIDE, lax.rem(j, SIDE)
        qx = lax.rem(px + SIDE + sign * dx, SIDE)
        qy = lax.rem(py + SIDE + sign * dy, SIDE)
        return qx * SIDE + qy

    def at_chip(i):
        return (z, 2 * chip(i, 1) + core)

    twin = (z, 2 * (px * SIDE + py) + other)

    ld_x = pltpu.make_async_copy(feat, xa.at[z], lsem.at[0])
    ld_a = pltpu.make_async_copy(vals, blk, lsem.at[1])
    ld_w = pltpu.make_async_copy(weight, w_v, lsem.at[2])
    ld_b = pltpu.make_async_copy(bias, b_v, lsem.at[3])
    ld_c = pltpu.make_async_copy(cot, c_v, lsem.at[4])
    for ld in (ld_x, ld_a, ld_w, ld_b, ld_c):
        ld.start()

    barrier = pltpu.get_barrier_semaphore()
    for off in (1, -1, 2, -2):
        pl.semaphore_signal(barrier, inc=1, device_id=at_z(off), device_id_type=MESH)
    pl.semaphore_signal(barrier, inc=1, device_id=twin, device_id_type=MESH)

    def greet(i, carry):
        pl.semaphore_signal(barrier, inc=1, device_id=at_chip(i), device_id_type=MESH)
        return carry

    lax.fori_loop(0, CHIPS - 1, greet, 0)

    prod[DEAD] = jnp.zeros((BLOCK, F_IN), F32)
    ga[NCOL] = jnp.zeros((F_IN, BLOCK), BF16)
    ld_x.wait()
    pl.semaphore_wait(barrier, 4 + 1 + CHIPS - 1)

    def invert(t, carry):
        ids = [adj[t, s] for s in range(SLOTS)]
        for k in range(NCOL):
            slot = jnp.int32(DEAD)
            for s in range(SLOTS):
                slot = jnp.where(ids[s] == k, t * SLOTS + s, slot)
            inv[t, k] = slot
        return carry

    def multiply(t):
        tall = blk[pl.ds(t * SLOTS, SLOTS)].reshape(SLOTS * BLOCK, BLOCK)
        out = jnp.dot(tall, xa[t], preferred_element_type=F32)
        prod[pl.ds(t * SLOTS, SLOTS)] = out.reshape(SLOTS, BLOCK, F_IN)

    sent = []
    arriving = {}
    for phase in range(4):
        for dist in (2 * phase + 1, 2 * phase + 2):
            for d in (1, -1):
                if dist == 8 and d == -1:
                    continue
                if phase == 0:
                    src, jump = ring(0), d * dist
                else:
                    arriving[d * (dist - 2)].wait_recv()
                    src, jump = ring(-d * (dist - 2)), 2 * d
                m = FAR_FIRST.index(d * dist)
                cp = remote(xa.at[src], xa.at[src], zs.at[m], zr.at[m], at_z(jump))
                cp.start()
                sent.append(cp)
                arriving[d * dist] = cp
        lax.fori_loop(4 * phase, 4 * phase + 4, invert, 0)
        if phase == 0:
            ld_a.wait()
            multiply(z)
        else:

            def multiply_pair(i, carry):
                dist = 2 * phase - 1 + i // 2
                multiply(ring((2 * lax.rem(i, 2) - 1) * dist))
                return carry

            lax.fori_loop(0, 4 if phase < 3 else 3, multiply_pair, 0)
    for off in (7, -7, -6, 8):
        arriving[off].wait_recv()
        multiply(ring(-off))

    def placed(k):
        total = prod[inv[0, k]]
        for t in range(1, NZ):
            total = total + prod[inv[t, k]]
        return total

    def to_twin(i, carry):
        sd[i] = placed(2 * chip(i, 1) + other).astype(BF16)
        remote(sd.at[i], rd.at[i], ds.at[i], dr.at[i], twin).start()
        return carry

    lax.fori_loop(0, CHIPS, to_twin, 0)

    def both(i):
        mine = placed(2 * chip(i, 1) + core)
        remote(sd.at[i], rd.at[i], ds.at[i], dr.at[i], twin).wait_recv()
        return mine + rd[i].astype(F32)

    def to_owner(i, carry):
        sz[i] = both(i).astype(BF16)
        remote(sz.at[i], rz.at[i], xs.at[i], xr.at[i], at_chip(i)).start()
        return carry

    lax.fori_loop(0, CHIPS - 1, to_owner, 0)
    own[0] = both(CHIPS - 1)

    def collect(i, carry):
        remote(sz.at[i], rz.at[i], xs.at[i], xr.at[i], at_chip(i)).wait_recv()
        own[0] += rz[i].astype(F32)
        return carry

    lax.fori_loop(0, CHIPS - 1, collect, 0)

    ld_w.wait()
    ld_b.wait()
    ld_c.wait()
    agg = own[0]
    agg_hi = agg.astype(BF16)
    agg_lo = (agg - agg_hi.astype(F32)).astype(BF16)
    w = w_v[...]
    hidden = jnp.dot(agg_hi, w, preferred_element_type=F32)
    hidden = hidden + jnp.dot(agg_lo, w, preferred_element_type=F32)
    preact = hidden + b_v[...]
    gate = jax.nn.sigmoid(preact)
    act_v[...] = (preact * gate).astype(BF16)
    st_act = pltpu.make_async_copy(act_v, act_out, lsem.at[5])
    st_act.start()
    dpre = c_v[...].astype(F32) * gate * (1.0 + preact * (1.0 - gate))
    dpre_round = dpre.astype(BF16)
    ga[c] = lax.dot_general(
        w, dpre_round, (((1,), (1,)), ((), ())), preferred_element_type=F32
    ).astype(BF16)

    def spread(i, carry):
        remote(ga.at[c], ga.at[c], gs.at[i], gr.at[i], at_chip(i)).start()
        return carry

    lax.fori_loop(0, CHIPS - 1, spread, 0)
    g_twin = remote(ga.at[c], ga.at[c], gs.at[CHIPS - 1], gr.at[CHIPS - 1], twin)
    g_twin.start()

    tn = (((0,), (0,)), ((), ()))
    dw = lax.dot_general(agg_hi, dpre_round, tn, preferred_element_type=F32)
    dw = dw + lax.dot_general(agg_lo, dpre_round, tn, preferred_element_type=F32)
    db = jnp.sum(dpre, axis=0, keepdims=True)
    first = lax.broadcasted_iota(jnp.int32, (8, F_OUT), 0) == 0
    db8 = jnp.where(first, jnp.broadcast_to(db, (8, F_OUT)), 0.0)
    for half in range(2):
        lanes = slice(half * 128, half * 128 + 128)
        dwp[half, 0:F_IN] = dw[:, lanes]
        dwp[half, F_IN : F_IN + 8] = db8[:, lanes]
    w_twin = remote(dwp.at[other], dwr, ws.at[0], wr.at[0], twin)
    w_twin.start()
    w_twin.wait_recv()
    for p in range(CHIPS):
        dwm[p, 0:8] = dwp[core, 8 * p : 8 * p + 8] + dwr[8 * p : 8 * p + 8]
    db_half = dwp[core, F_IN : F_IN + 8] + dwr[F_IN : F_IN + 8]
    for p in range(CHIPS):
        dwm[p, 8:16] = db_half

    def w_spread(i, carry):
        remote(dwm.at[chip(i, 1)], dwx.at[i], wxs.at[i], wxr.at[i], at_chip(i)).start()
        return carry

    lax.fori_loop(0, CHIPS - 1, w_spread, 0)

    def forward(i, carry):
        src = 2 * chip(i, -1) + core
        remote(ga.at[src], ga.at[src], gs.at[i], gr.at[i], at_chip(i)).wait_recv()
        remote(ga.at[src], ga.at[src], fs.at[i], fr.at[i], twin).start()
        return carry

    lax.fori_loop(0, CHIPS - 1, forward, 0)

    dwz[z] = dwm[px * SIDE + py]

    def w_collect(i, carry):
        remote(dwm.at[0], dwx.at[i], wxs.at[i], wxr.at[i], at_chip(i)).wait_recv()
        dwz[z] += dwx[i]
        return carry

    lax.fori_loop(0, CHIPS - 1, w_collect, 0)

    def w_ring(i):
        return remote(dwz.at[z], dwz.at[z], wzs.at[i], wzr.at[i], at_z(i + 1))

    def w_ring_start(i, carry):
        w_ring(i).start()
        return carry

    lax.fori_loop(0, NZ - 1, w_ring_start, 0)

    g_twin.wait_recv()

    def from_twin(i, carry):
        src = 2 * chip(i, -1) + other
        remote(ga.at[src], ga.at[src], fs.at[i], fr.at[i], twin).wait_recv()
        return carry

    lax.fori_loop(0, CHIPS - 1, from_twin, 0)

    def pull(i, carry):
        q, r = i // 4, lax.rem(i, 4)
        t = ring(-jnp.where(r < 2, 8 - 2 * q - r, 7 + 2 * q + r))
        picks = []
        for s in range(SLOTS):
            k = adj[t, s]
            picks.append(ga[jnp.where(k < 0, NCOL, k)])
        wide = jnp.concatenate(picks, axis=1)
        tall = blk[pl.ds(t * SLOTS, SLOTS)].reshape(SLOTS * BLOCK, BLOCK)
        own[i] = jnp.dot(wide, tall, preferred_element_type=F32)
        return carry

    def b_copy(m):
        b = FAR_FIRST[m]
        return remote(sb.at[m], rb.at[m], bs.at[m], br.at[m], at_z(toward(b) - b))

    def reduce_group(phase):
        for m in range(4 * phase, min(4 * phase + 4, NZ - 1)):
            far = behind(FAR_FIRST[m])
            if far is None:
                sb[m] = own[m].astype(BF16)
            else:
                n = FAR_FIRST.index(far)
                b_copy(n).wait_recv()
                sb[m] = (own[m] + rb[n].astype(F32)).astype(BF16)
            b_copy(m).start()

    lax.fori_loop(0, 4, pull, 0)
    reduce_group(0)
    lax.fori_loop(4, 16, pull, 0)
    reduce_group(1)
    reduce_group(2)

    def w_sum(i, total):
        w_ring(i).wait_recv()
        return total

    lax.fori_loop(0, NZ - 1, w_sum, 0)
    piece = dwz[0]
    for t in range(1, NZ):
        piece = piece + dwz[t]
    me = px * SIDE + py
    dwf[core, CHIPS] = piece[8:16]
    dwf[core, me] = piece[0:8]

    def w_gather(i, src):
        return remote(
            dwf.at[core, src], dwf.at[core, src], was.at[i], war.at[i], at_chip(i)
        )

    def w_gather_start(i, carry):
        w_gather(i, me).start()
        return carry

    lax.fori_loop(0, CHIPS - 1, w_gather_start, 0)

    reduce_group(3)

    def w_gather_wait(i, carry):
        w_gather(i, chip(i, -1)).wait_recv()
        return carry

    lax.fori_loop(0, CHIPS - 1, w_gather_wait, 0)
    w_back = remote(dwf.at[core], dwf.at[core], ws.at[1], wr.at[1], twin)
    w_back.start()

    total = own[NZ - 1]
    for b in (2, 1, -1, -2):
        n = FAR_FIRST.index(b)
        b_copy(n).wait_recv()
        total = total + rb[n].astype(F32)
    df_v[...] = total.T.astype(BF16)
    st_df = pltpu.make_async_copy(df_v, df_out, lsem.at[6])
    st_df.start()

    w_in = remote(dwf.at[other], dwf.at[other], ws.at[1], wr.at[1], twin)
    w_in.wait_recv()
    for half in range(2):
        lanes = slice(half * 128, half * 128 + 128)
        dwo[:, lanes] = dwf[half, 0:CHIPS].reshape(F_IN, 128)
        dbo[:, lanes] = dwf[half, CHIPS, 0:1]
    st_dw = pltpu.make_async_copy(dwo, dw_out, lsem.at[7])
    st_dw.start()
    st_db = pltpu.make_async_copy(dbo, db_out, lsem.at[8])
    st_db.start()

    for cp in sent:
        cp.wait_send()

    def drain(i, carry):
        remote(sd.at[i], rd.at[i], ds.at[i], dr.at[i], twin).wait_send()
        remote(ga.at[c], ga.at[c], gs.at[i], gr.at[i], twin).wait_send()
        return carry

    lax.fori_loop(0, CHIPS, drain, 0)

    def drain_15(i, carry):
        remote(sz.at[i], rz.at[i], xs.at[i], xr.at[i], twin).wait_send()
        remote(ga.at[c], ga.at[c], fs.at[i], fr.at[i], twin).wait_send()
        remote(dwm.at[0], dwx.at[i], wxs.at[i], wxr.at[i], twin).wait_send()
        remote(dwz.at[z], dwz.at[z], wzs.at[i], wzr.at[i], twin).wait_send()
        w_gather(i, me).wait_send()
        remote(sb.at[i], rb.at[i], bs.at[i], br.at[i], twin).wait_send()
        return carry

    lax.fori_loop(0, CHIPS - 1, drain_15, 0)
    w_twin.wait_send()
    w_back.wait_send()
    for st in (st_act, st_df, st_dw, st_db):
        st.wait()


def local(features, weight, bias, adj_values, adj_rows, cotangent):
    any_space = pl.BlockSpec(memory_space=pl.ANY)
    dma = pltpu.SemaphoreType.DMA
    outs = pl.pallas_call(
        kernel,
        out_shape=(
            jax.ShapeDtypeStruct((BLOCK, F_OUT), BF16),
            jax.ShapeDtypeStruct((BLOCK, F_IN), BF16),
            jax.ShapeDtypeStruct((F_IN, F_OUT), F32),
            jax.ShapeDtypeStruct((1, F_OUT), F32),
        ),
        in_specs=[pl.BlockSpec(memory_space=pltpu.SMEM)] + [any_space] * 5,
        out_specs=[any_space] * 4,
        scratch_shapes=[
            pltpu.VMEM((NZ, BLOCK, F_IN), BF16),
            pltpu.VMEM((DEAD, BLOCK, BLOCK), BF16),
            pltpu.VMEM((DEAD + 1, BLOCK, F_IN), F32),
            pltpu.SMEM((NZ, NCOL), jnp.int32),
            pltpu.VMEM((F_IN, F_OUT), BF16),
            pltpu.VMEM((1, F_OUT), F32),
            pltpu.VMEM((BLOCK, F_OUT), BF16),
            pltpu.VMEM((BLOCK, F_OUT), BF16),
            pltpu.VMEM((CHIPS, BLOCK, F_IN), BF16),
            pltpu.VMEM((CHIPS, BLOCK, F_IN), BF16),
            pltpu.VMEM((CHIPS - 1, BLOCK, F_IN), BF16),
            pltpu.VMEM((CHIPS - 1, BLOCK, F_IN), BF16),
            pltpu.VMEM((NCOL + 1, F_IN, BLOCK), BF16),
            pltpu.VMEM((NZ, F_IN, BLOCK), F32),
            pltpu.VMEM((NZ - 1, F_IN, BLOCK), BF16),
            pltpu.VMEM((NZ - 1, F_IN, BLOCK), BF16),
            pltpu.VMEM((BLOCK, F_IN), BF16),
            pltpu.VMEM((2, F_IN + 8, 128), F32),
            pltpu.VMEM((F_IN + 8, 128), F32),
            pltpu.VMEM((CHIPS, 16, 128), F32),
            pltpu.VMEM((CHIPS - 1, 16, 128), F32),
            pltpu.VMEM((NZ, 16, 128), F32),
            pltpu.VMEM((2, CHIPS + 1, 8, 128), F32),
            pltpu.VMEM((F_IN, F_OUT), F32),
            pltpu.VMEM((1, F_OUT), F32),
            dma((9,)),
            dma((15,)), dma((15,)),
            dma((16,)), dma((16,)),
            dma((15,)), dma((15,)),
            dma((16,)), dma((16,)),
            dma((15,)), dma((15,)),
            dma((15,)), dma((15,)),
            dma((2,)), dma((2,)),
            dma((15,)), dma((15,)),
            dma((15,)), dma((15,)),
            dma((15,)), dma((15,)),
        ],
        compiler_params=pltpu.CompilerParams(
            collective_id=0, has_side_effects=True, vmem_limit_bytes=56 << 20
        ),
    )(
        adj_rows[0],
        features,
        weight,
        bias.reshape(1, F_OUT),
        adj_values.reshape(DEAD, BLOCK, BLOCK),
        cotangent,
    )
    activations, dfeatures, dweight, dbias = outs
    return activations, dfeatures, dweight, dbias.reshape(F_OUT)


def solution(mesh):
    return jax.shard_map(
        local,
        mesh=mesh,
        in_specs=(
            P(("row", "col"), None),
            P(),
            P(),
            P("row", "col", None, None, None),
            P("row", "col", None),
            P(("row", "col"), None),
        ),
        out_specs=(P(("row", "col"), None), P(("row", "col"), None), P(), P()),
        check_vma=False,
    )
```

time: 881 us -> 88.9 us (0.10)
  waiting for transfers between devices: 679 us -> 0 us
  blocking collectives: 104 us -> 0 us
  Pallas kernels: 0 us -> 81 us
  local copies, waits for them, and re-layouts: 42.8 us -> 6.97 us
  other arithmetic: 25.8 us -> 0 us
  matrix products: 15.2 us -> 0 us
  between operations: 13.9 us -> 0.64 us
    psum x1 -> x0, waiting for transfers between devices: 442 us -> none  [local(): dweight, dbias = lax.psum((weight_local, bias_local), ('row', 'col'))]
    all_gather x2 -> x0, waiting for transfers between devices: 130 us -> none  [the longest x1 67.6 us: local(): column_list = lax.all_gather(transformed, 'row', axis=0, tiled=True)]
    reduce_scatter x2 -> x0, waiting for transfers between devices: 107 us -> none  [the longest x1 107 us: local(): lax.psum_scatter(placed.reshape(row_blocks * BLOCK, F_OUT).astype(jnp.bfl...]
    psum x1 -> x0, blocking collectives: 104 us -> none  [local(): dweight, dbias = lax.psum((weight_local, bias_local), ('row', 'col'))]
    pallas_call x0 -> x1, Pallas kernels: none -> 81 us  [local(): pl.pallas_call(kernel, out_shape=(jax.ShapeDtypeStruct((BLOCK, F_OUT), BF...]
    scatter-add x1 -> x0, other arithmetic: 20.5 us -> none  [local(): placed = jax.ops.segment_sum(products, local_ids, num_segments=row_blocks)]
    dot_general x5 -> x0, matrix products: 15.2 us -> none  [the longest x1 7.6 us: local(): jnp.einsum('tsij,tjf->tsif', blocks, column_list.reshape(block_count_tota...]
    gather x1 -> x0, local copies, waits for them, and re-layouts: 14.4 us -> none  [local(): picked = jnp.take(grad_flat, live_ids, axis=0, mode='fill', fill_value=0)]
  transfers between devices with their start and end apart: 5 -> 0, of which waited for: 4 -> 0; matrix products, arithmetic and copies ran while one was open for 0% -> 0% of each run, Pallas kernels for 0% -> 0%
where the time goes in v1:
time: 88.9 us; the launch traced here: 88.6 us
  Pallas kernels  81 us (91%)
  local copies, waits for them, and re-layouts  6.97 us (8%)
    pallas_call x1, Pallas kernels, local(): pl.pallas_call(kernel, out_shape=(jax.ShapeDtypeStruct((BLOCK, F_OUT), BF...  81 us
    unnamed x4, local copies, waits for them, and re-layouts  5.61 us

profile of v1, /device:TPU:1, one launch (start us, length us, event | category | flops | bytes accessed | tf_op | source)
XLA Modules:
  0.0 88.6 jit_solution(17035716401405791356)
XLA Ops:
  0.6 1.4 %copy.11 = s32[1,16,6]{2,1,0:T(8,128)} copy(s32[1,16,6]{1,0,2:T(1,128)} %param.10) | data formatting | bytes 768 | tf_op jit(solution)/shard_map/squeeze | solution.py:436
  2.0 81.0 %shard_map.93 = (bf16[128,256]{1,0:T(8,128)(2,1)}, bf16[128,128]{1,0:T(8,128)(2,1)}, f32[128,256]{1,0:T(8,128)}, f32[1,256]{1,0:T(1,128)}) custom-call(s32[16,6]{1,0:T(8,128)} %bitcast.5, bf16[128,128]{1,0:T(8,128)(2,1)} %feat.1, bf16[128,256]{1,0:T(8,128)(2,1)} %weight.1, f32[1,256]{1,0:T(1,128)} %bitcast.6, bf16[96,128,128]{2,1,0:T(8,128)(2,1)} %bitcast.4, ...), custom_call_target="tpu_custom_call" | custom-call | tf_op jit(solution)/shard_map/pallas_call | solution.py:384
  83.0 1.5 %copy.16 = bf16[128,256]{1,0:T(8,128)(2,1)} copy(bf16[128,256]{1,0:T(8,128)(2,1)} %get-tuple-element.16) | data formatting | bytes 131072
  84.4 1.4 %copy.17 = bf16[128,128]{1,0:T(8,128)(2,1)} copy(bf16[128,128]{1,0:T(8,128)(2,1)} %get-tuple-element.17) | data formatting | bytes 65536
  85.8 1.6 %copy.18 = f32[128,256]{1,0:T(8,128)} copy(f32[128,256]{1,0:T(8,128)} %get-tuple-element.18) | data formatting | bytes 262144
  87.4 1.2 %copy.19 = f32[256]{0:T(256)} copy(f32[256]{0:T(256)} %bitcast.7) | data formatting | bytes 2048

commit v2 on v1

v2 whole, which is shorter than its diff:
```python
import jax
import jax.numpy as jnp
from jax import lax
from jax.experimental import pallas as pl
from jax.experimental.pallas import tpu as pltpu
from jax.sharding import PartitionSpec as P

MESH = pl.DeviceIdType.MESH
BF16 = jnp.bfloat16
F32 = jnp.float32
BLOCK = 128
F_IN = 128
F_OUT = 256
SLOTS = 6
NZ = 16
SIDE = 4
CHIPS = SIDE * SIDE
NCOL = 2 * CHIPS
DEAD = NZ * SLOTS
LAG = 5
HALFWAY = 0
GATHER = (
    ((0, 3), (0, -3), (0, 1), (0, -1)),
    ((3, 6), (-3, -6), (1, 2), (-1, -2), (3, 4), (-3, -4)),
    ((6, 8), (6, 7), (-6, -7), (6, 5), (-6, -5)),
)
REDUCE = (
    ((8, 6), (7, 6), (-7, -6), (5, 6), (-5, -6), (4, 3), (-4, -3), (1, 0), (-1, 0)),
    ((6, 3), (-6, -3), (2, 0), (-2, 0)),
    ((3, 0), (-3, 0)),
)


def remote(src, dst, send_sem, recv_sem, device):
    return pltpu.make_async_remote_copy(
        src_ref=src,
        dst_ref=dst,
        send_sem=send_sem,
        recv_sem=recv_sem,
        device_id=device,
        device_id_type=MESH,
    )


def kernel(
    adj, feat, weight, bias, vals, cot,
    act_out, df_out, dw_out, db_out,
    xa, blk, prod, inv, w_v, b_v, c_v, act_v,
    sd, rd, sz, rz, ga, own, sb, rb, df_v,
    dwm, dwx, dwt, dwz, dwf, dwo, dbo,
    lsem, asem, zs, zr, ds, dr, xs, xr, gs, gr, fs, fr, bs, br, ws, wr,
    wxs, wxr, wzs, wzr, was, war,
):
    z = lax.axis_index("row")
    c = lax.axis_index("col")
    px, py, core = c // 8, (c // 2) % 4, c % 2
    other = 1 - core

    def ring(off):
        return lax.rem(z + (off + 2 * NZ), NZ)

    def at_z(off):
        return (ring(off), c)

    def far_first(a):
        return jnp.where(a == 0, 2, jnp.where(a == 1, 1, jnp.where(a == 2, 3, 0)))

    def chip(i, sign):
        dx, dy = far_first(i // SIDE), far_first(lax.rem(i, SIDE))
        qx = lax.rem(px + SIDE + sign * dx, SIDE)
        qy = lax.rem(py + SIDE + sign * dy, SIDE)
        return qx * SIDE + qy

    def at_chip(i):
        return (z, 2 * chip(i, 1) + core)

    twin = (z, 2 * (px * SIDE + py) + other)

    ld_x = pltpu.make_async_copy(feat, xa.at[z], lsem.at[0])
    ld_w = pltpu.make_async_copy(weight, w_v, lsem.at[2])
    ld_b = pltpu.make_async_copy(bias, b_v, lsem.at[3])
    ld_c = pltpu.make_async_copy(cot, c_v, lsem.at[4])

    def ld_a(t):
        part = pl.ds(t * SLOTS, SLOTS)
        return pltpu.make_async_copy(vals.at[part], blk.at[part], asem.at[t])

    def ld_a_start(t, carry):
        ld_a(t).start()
        return carry

    barrier = pltpu.get_barrier_semaphore()
    for off in (3, -3, 1, -1):
        pl.semaphore_signal(barrier, inc=1, device_id=at_z(off), device_id_type=MESH)
    ld_x.start()

    def greet(i, carry):
        pl.semaphore_signal(barrier, inc=1, device_id=at_chip(i), device_id_type=MESH)
        return carry

    lax.fori_loop(0, CHIPS - 1, greet, 0)
    pl.semaphore_signal(barrier, inc=1, device_id=twin, device_id_type=MESH)

    prod[DEAD] = jnp.zeros((BLOCK, F_IN), F32)
    ga[NCOL] = jnp.zeros((F_IN, BLOCK), BF16)
    ld_x.wait()
    pl.semaphore_wait(barrier, 4 + 1 + CHIPS - 1)

    def invert(t, carry):
        ids = [adj[s, 0, t] for s in range(SLOTS)]
        for k in range(NCOL):
            slot = jnp.int32(DEAD)
            for s in range(SLOTS):
                slot = jnp.where(ids[s] == k, t * SLOTS + s, slot)
            inv[t, k] = slot
        return carry

    def multiply(t):
        ld_a(t).wait()
        tall = blk[pl.ds(t * SLOTS, SLOTS)].reshape(SLOTS * BLOCK, BLOCK)
        out = jnp.dot(tall, xa[t], preferred_element_type=F32)
        prod[pl.ds(t * SLOTS, SLOTS)] = out.reshape(SLOTS, BLOCK, F_IN)

    def hop(a, b):
        block = xa.at[ring(-a)]
        return remote(block, block, zs.at[b % NZ], zr.at[b % NZ], at_z(b - a))

    here = {0}

    def arrive(b):
        if b not in here:
            hop(0, b).wait_recv()
            here.add(b)

    for stage, edges in enumerate(GATHER):
        for a, b in edges:
            arrive(a)
            hop(a, b).start()
        if stage == 0:
            lax.fori_loop(0, NZ, ld_a_start, 0)
            for ld in (ld_w, ld_b, ld_c):
                ld.start()
        if stage < 2:
            lax.fori_loop(8 * stage, 8 * stage + 8, invert, 0)
        if stage == 1:
            for b in (0, 1, -1, 3, -3):
                multiply(ring(-b))
        if stage == 2:
            for b in (6, -6, 2, -2, 4, -4, 5, -5, 7, -7, 8):
                arrive(b)
                multiply(ring(-b))

    def placed(k):
        total = prod[inv[0, k]]
        for t in range(1, NZ):
            total = total + prod[inv[t, k]]
        return total

    def to_twin(i, carry):
        sd[i] = placed(2 * chip(i, 1) + other).astype(BF16)
        remote(sd.at[i], rd.at[i], ds.at[i], dr.at[i], twin).start()
        return carry

    def both(i):
        mine = placed(2 * chip(i, 1) + core)
        remote(sd.at[i], rd.at[i], ds.at[i], dr.at[i], twin).wait_recv()
        return mine + rd[i].astype(F32)

    def to_owner(i, carry):
        sz[i] = both(i).astype(BF16)
        remote(sz.at[i], rz.at[i], xs.at[i], xr.at[i], at_chip(i)).start()
        return carry

    def to_both(i, carry):
        to_twin(i, carry)
        return to_owner(i - LAG, carry)

    lax.fori_loop(0, LAG, to_twin, 0)
    lax.fori_loop(LAG, CHIPS, to_both, 0)
    lax.fori_loop(CHIPS - LAG, CHIPS - 1, to_owner, 0)
    own[0] = both(CHIPS - 1)

    def collect(i, carry):
        remote(sz.at[i], rz.at[i], xs.at[i], xr.at[i], at_chip(i)).wait_recv()
        own[0] += rz[i].astype(F32)
        return carry

    lax.fori_loop(0, CHIPS - 1, collect, 0)

    ld_w.wait()
    ld_b.wait()
    ld_c.wait()
    agg = own[0]
    agg_hi = agg.astype(BF16)
    agg_lo = (agg - agg_hi.astype(F32)).astype(BF16)
    w = w_v[...]
    hidden = jnp.dot(agg_hi, w, preferred_element_type=F32)
    hidden = hidden + jnp.dot(agg_lo, w, preferred_element_type=F32)
    preact = hidden + b_v[...]
    gate = jax.nn.sigmoid(preact)
    act_v[...] = (preact * gate).astype(BF16)
    st_act = pltpu.make_async_copy(act_v, act_out, lsem.at[5])
    st_act.start()
    dpre = c_v[...].astype(F32) * gate * (1.0 + preact * (1.0 - gate))
    dpre_round = dpre.astype(BF16)
    ga[c] = lax.dot_general(
        w, dpre_round, (((1,), (1,)), ((), ())), preferred_element_type=F32
    ).astype(BF16)

    tn = (((0,), (0,)), ((), ()))
    dw = lax.dot_general(agg_hi, dpre_round, tn, preferred_element_type=F32)
    dw = dw + lax.dot_general(agg_lo, dpre_round, tn, preferred_element_type=F32)
    db = jnp.sum(dpre, axis=0, keepdims=True)
    first = lax.broadcasted_iota(jnp.int32, (8, F_OUT), 0) == 0
    db8 = jnp.where(first, jnp.broadcast_to(db, (8, F_OUT)), 0.0)
    for p in range(CHIPS):
        both_parts = jnp.concatenate([dw[8 * p : 8 * p + 8], db8], axis=0)
        dwm[p] = both_parts.astype(BF16)

    def w_spread(i, carry):
        remote(dwm.at[chip(i, 1)], dwx.at[i], wxs.at[i], wxr.at[i], at_chip(i)).start()
        return carry

    lax.fori_loop(0, CHIPS - 1, w_spread, 0)

    def spread(i, carry):
        remote(ga.at[c], ga.at[c], gs.at[i], gr.at[i], at_chip(i)).start()
        return carry

    lax.fori_loop(0, CHIPS - 1, spread, 0)
    g_twin = remote(ga.at[c], ga.at[c], gs.at[CHIPS - 1], gr.at[CHIPS - 1], twin)
    g_twin.start()

    def w_collect(i, total):
        remote(dwm.at[0], dwx.at[i], wxs.at[i], wxr.at[i], at_chip(i)).wait_recv()
        return total + dwx[i].astype(F32)

    me = px * SIDE + py
    mixed = lax.fori_loop(0, CHIPS - 1, w_collect, dwm[me].astype(F32))
    left, right = mixed[:, 0:128], mixed[:, 128:F_OUT]
    dwt[0] = jnp.where(core == 0, right, left)
    w_twin = remote(dwt.at[0], dwt.at[1], ws.at[0], wr.at[0], twin)
    w_twin.start()

    def forward(i, carry):
        src = 2 * chip(i, -1) + core
        remote(ga.at[src], ga.at[src], gs.at[i], gr.at[i], at_chip(i)).wait_recv()
        remote(ga.at[src], ga.at[src], fs.at[i], fr.at[i], twin).start()
        return carry

    lax.fori_loop(0, HALFWAY, forward, 0)
    w_twin.wait_recv()
    dwz[z] = (jnp.where(core == 0, left, right) + dwt[1]).astype(BF16)

    def w_ring(i):
        return remote(dwz.at[z], dwz.at[z], wzs.at[i], wzr.at[i], at_z(i + 1))

    def w_ring_start(i, carry):
        w_ring(i).start()
        return carry

    lax.fori_loop(0, NZ - 1, w_ring_start, 0)
    lax.fori_loop(HALFWAY, CHIPS - 1, forward, 0)

    g_twin.wait_recv()

    def from_twin(i, carry):
        src = 2 * chip(i, -1) + other
        remote(ga.at[src], ga.at[src], fs.at[i], fr.at[i], twin).wait_recv()
        return carry

    lax.fori_loop(0, CHIPS - 1, from_twin, 0)

    def pull(i, carry):
        t = ring(-i)
        picks = []
        for s in range(SLOTS):
            k = adj[s, 0, t]
            picks.append(ga[jnp.where(k < 0, NCOL, k)])
        wide = jnp.concatenate(picks, axis=1)
        tall = blk[pl.ds(t * SLOTS, SLOTS)].reshape(SLOTS * BLOCK, BLOCK)
        own[i] = jnp.dot(wide, tall, preferred_element_type=F32)
        return carry

    def back(a, b):
        n = a % NZ
        return remote(sb.at[n], rb.at[n], bs.at[n], br.at[n], at_z(b - a))

    def summed(b):
        total = own[b % NZ]
        for edges in REDUCE:
            for a, to in edges:
                if to == b:
                    back(a, b).wait_recv()
                    total = total + rb[a % NZ].astype(F32)
        return total

    for a, b in REDUCE[0]:
        pull(a % NZ, 0)
        sb[a % NZ] = own[a % NZ].astype(BF16)
        back(a, b).start()
    for edges in REDUCE[1:]:
        for a, b in edges:
            pull(a % NZ, 0)
    pull(0, 0)
    for edges in REDUCE[1:]:
        for a, b in edges:
            sb[a % NZ] = summed(a).astype(BF16)
            back(a, b).start()

    def w_sum(i, total):
        w_ring(i).wait_recv()
        return total

    lax.fori_loop(0, NZ - 1, w_sum, 0)
    piece = dwz[0].astype(F32)
    for t in range(1, NZ):
        piece = piece + dwz[t].astype(F32)
    dwf[core, CHIPS] = piece[8:16]
    dwf[core, me] = piece[0:8]

    def w_gather(i, src):
        return remote(
            dwf.at[core, src], dwf.at[core, src], was.at[i], war.at[i], at_chip(i)
        )

    def w_gather_start(i, carry):
        w_gather(i, me).start()
        return carry

    lax.fori_loop(0, CHIPS - 1, w_gather_start, 0)

    total = summed(0)
    df_v[...] = total.T.astype(BF16)
    st_df = pltpu.make_async_copy(df_v, df_out, lsem.at[6])
    st_df.start()

    def w_gather_wait(i, carry):
        w_gather(i, chip(i, -1)).wait_recv()
        return carry

    lax.fori_loop(0, CHIPS - 1, w_gather_wait, 0)
    w_back = remote(dwf.at[core], dwf.at[core], ws.at[1], wr.at[1], twin)
    w_back.start()

    w_in = remote(dwf.at[other], dwf.at[other], ws.at[1], wr.at[1], twin)
    w_in.wait_recv()
    for half in range(2):
        lanes = slice(half * 128, half * 128 + 128)
        dwo[:, lanes] = dwf[half, 0:CHIPS].reshape(F_IN, 128)
        dbo[:, lanes] = dwf[half, CHIPS, 0:1]
    st_dw = pltpu.make_async_copy(dwo, dw_out, lsem.at[7])
    st_dw.start()
    st_db = pltpu.make_async_copy(dbo, db_out, lsem.at[8])
    st_db.start()

    def drain(i, carry):
        remote(sd.at[i], rd.at[i], ds.at[i], dr.at[i], twin).wait_send()
        remote(ga.at[c], ga.at[c], gs.at[i], gr.at[i], twin).wait_send()
        return carry

    lax.fori_loop(0, CHIPS, drain, 0)

    def drain_15(i, carry):
        remote(sz.at[i], rz.at[i], xs.at[i], xr.at[i], twin).wait_send()
        remote(ga.at[c], ga.at[c], fs.at[i], fr.at[i], twin).wait_send()
        remote(dwm.at[0], dwx.at[i], wxs.at[i], wxr.at[i], twin).wait_send()
        remote(dwz.at[z], dwz.at[z], wzs.at[i], wzr.at[i], twin).wait_send()
        w_gather(i, me).wait_send()
        remote(xa.at[z], xa.at[z], zs.at[i + 1], zr.at[i + 1], twin).wait_send()
        remote(sb.at[i], rb.at[i], bs.at[i + 1], br.at[i + 1], twin).wait_send()
        return carry

    lax.fori_loop(0, CHIPS - 1, drain_15, 0)
    w_twin.wait_send()
    w_back.wait_send()
    for st in (st_act, st_df, st_dw, st_db):
        st.wait()


def hand_over(*refs):
    n = len(refs) // 2
    sem = refs[-1]
    moves = [
        pltpu.make_async_copy(refs[i], refs[n + i], sem.at[i]) for i in range(n)
    ]
    for move in moves:
        move.start()
    for move in moves:
        move.wait()


def local(features, weight, bias, adj_values, adj_rows, cotangent):
    any_space = pl.BlockSpec(memory_space=pl.ANY)
    dma = pltpu.SemaphoreType.DMA
    outs = pl.pallas_call(
        kernel,
        out_shape=(
            jax.ShapeDtypeStruct((BLOCK, F_OUT), BF16),
            jax.ShapeDtypeStruct((BLOCK, F_IN), BF16),
            jax.ShapeDtypeStruct((F_IN, F_OUT), F32),
            jax.ShapeDtypeStruct((1, F_OUT), F32),
        ),
        in_specs=[pl.BlockSpec(memory_space=pltpu.SMEM)] + [any_space] * 5,
        out_specs=[any_space] * 4,
        scratch_shapes=[
            pltpu.VMEM((NZ, BLOCK, F_IN), BF16),
            pltpu.VMEM((DEAD, BLOCK, BLOCK), BF16),
            pltpu.VMEM((DEAD + 1, BLOCK, F_IN), F32),
            pltpu.SMEM((NZ, NCOL), jnp.int32),
            pltpu.VMEM((F_IN, F_OUT), BF16),
            pltpu.VMEM((1, F_OUT), F32),
            pltpu.VMEM((BLOCK, F_OUT), BF16),
            pltpu.VMEM((BLOCK, F_OUT), BF16),
            pltpu.VMEM((CHIPS, BLOCK, F_IN), BF16),
            pltpu.VMEM((CHIPS, BLOCK, F_IN), BF16),
            pltpu.VMEM((CHIPS - 1, BLOCK, F_IN), BF16),
            pltpu.VMEM((CHIPS - 1, BLOCK, F_IN), BF16),
            pltpu.VMEM((NCOL + 1, F_IN, BLOCK), BF16),
            pltpu.VMEM((NZ, F_IN, BLOCK), F32),
            pltpu.VMEM((NZ, F_IN, BLOCK), BF16),
            pltpu.VMEM((NZ, F_IN, BLOCK), BF16),
            pltpu.VMEM((BLOCK, F_IN), BF16),
            pltpu.VMEM((CHIPS, 16, F_OUT), BF16),
            pltpu.VMEM((CHIPS - 1, 16, F_OUT), BF16),
            pltpu.VMEM((2, 16, 128), F32),
            pltpu.VMEM((NZ, 16, 128), BF16),
            pltpu.VMEM((2, CHIPS + 1, 8, 128), F32),
            pltpu.VMEM((F_IN, F_OUT), F32),
            pltpu.VMEM((1, F_OUT), F32),
            dma((9,)),
            dma((16,)),
            dma((16,)), dma((16,)),
            dma((16,)), dma((16,)),
            dma((15,)), dma((15,)),
            dma((16,)), dma((16,)),
            dma((15,)), dma((15,)),
            dma((16,)), dma((16,)),
            dma((2,)), dma((2,)),
            dma((15,)), dma((15,)),
            dma((15,)), dma((15,)),
            dma((15,)), dma((15,)),
        ],
        compiler_params=pltpu.CompilerParams(
            collective_id=0, has_side_effects=True, vmem_limit_bytes=56 << 20
        ),
    )(
        jnp.transpose(adj_rows, (2, 0, 1)),
        features,
        weight,
        bias.reshape(1, F_OUT),
        adj_values.reshape(DEAD, BLOCK, BLOCK),
        cotangent,
    )
    activations, dfeatures, dweight, dbias = pl.pallas_call(
        hand_over,
        out_shape=tuple(jax.ShapeDtypeStruct(o.shape, o.dtype) for o in outs),
        in_specs=[pl.BlockSpec(memory_space=pltpu.VMEM)] * 4,
        out_specs=[any_space] * 4,
        scratch_shapes=[dma((4,))],
    )(*outs)
    return activations, dfeatures, dweight, dbias.reshape(F_OUT)


def solution(mesh):
    return jax.shard_map(
        local,
        mesh=mesh,
        in_specs=(
            P(("row", "col"), None),
            P(),
            P(),
            P("row", "col", None, None, None),
            P("row", "col", None),
            P(("row", "col"), None),
        ),
        out_specs=(P(("row", "col"), None), P(("row", "col"), None), P(), P()),
        check_vma=False,
    )
```

time: 88.9 us -> 77.2 us (0.87)
  local copies, waits for them, and re-layouts: 6.97 us -> 0 us
  Pallas kernels: 81 us -> 76.4 us
    pallas_call x1, Pallas kernels: 81 us -> 74.7 us  [local(): pl.pallas_call(kernel, out_shape=(jax.ShapeDtypeStruct((BLOCK, F_OUT), BF...]
    unnamed x4 -> x0, local copies, waits for them, and re-layouts: 5.61 us -> none
    pallas_call x0 -> x1, Pallas kernels: none -> 1.69 us  [local(): pl.pallas_call(hand_over, out_shape=tuple((jax.ShapeDtypeStruct(o.shape,...]
    squeeze x1 -> x0, local copies, waits for them, and re-layouts: 1.36 us -> none  [local(): adj_rows[0]]
where the time goes in v2:
time: 77.2 us; the launch traced here: 77 us
  Pallas kernels  76.4 us (99%)
    pallas_call x1, Pallas kernels, local(): pl.pallas_call(kernel, out_shape=(jax.ShapeDtypeStruct((BLOCK, F_OUT), BF...  74.7 us
    pallas_call x1, Pallas kernels, local(): pl.pallas_call(hand_over, out_shape=tuple((jax.ShapeDtypeStruct(o.shape,...  1.69 us

profile of v2, /device:TPU:1, one launch (start us, length us, event | category | flops | bytes accessed | tf_op | source)
XLA Modules:
  0.0 77.0 jit_solution(1188638745884867950)
XLA Ops:
  0.6 74.7 %shard_map.93 = (bf16[128,256]{1,0:T(8,128)(2,1)}, bf16[128,128]{1,0:T(8,128)(2,1)}, f32[128,256]{1,0:T(8,128)}, f32[1,256]{1,0:T(1,128)}) custom-call(s32[6,1,16]{2,1,0:T(1,128)} %bitcast.5, bf16[128,128]{1,0:T(8,128)(2,1)} %feat.1, bf16[128,256]{1,0:T(8,128)(2,1)} %weight.1, f32[1,256]{1,0:T(1,128)} %bitcast.6, bf16[96,128,128]{2,1,0:T(8,128)(2,1)} %bitcast.4, ...), custom_call_target="tpu_custom_call" | custom-call | tf_op jit(solution)/shard_map/pallas_call | solution.py:396
  75.3 1.7 %shard_map.94 = (bf16[128,256]{1,0:T(8,128)(2,1)}, bf16[128,128]{1,0:T(8,128)(2,1)}, f32[128,256]{1,0:T(8,128)}, f32[1,256]{1,0:T(1,128)}) custom-call(bf16[128,256]{1,0:T(8,128)(2,1)} %get-tuple-element.12.refs_0_, bf16[128,128]{1,0:T(8,128)(2,1)} %get-tuple-element.13.refs_1_, f32[128,256]{1,0:T(8,128)} %get-tuple-element.14.refs_2_, ...), custom_call_target="tpu_custom_call" | custom-call | tf_op jit(solution)/shard_map/pallas_call | solution.py:455

commit v3 on v2

--- a/solution.py
+++ b/solution.py
@@ -17,7 +17,7 @@
 CHIPS = SIDE * SIDE
 NCOL = 2 * CHIPS
 DEAD = NZ * SLOTS
-LAG = 5
+LAG = 2
 HALFWAY = 0
 GATHER = (
     ((0, 3), (0, -3), (0, 1), (0, -1)),
@@ -43,9 +43,9 @@
 
 
 def kernel(
-    adj, feat, weight, bias, vals, cot,
+    ids, feat, weight, bias, vals, cot,
     act_out, df_out, dw_out, db_out,
-    xa, blk, prod, inv, w_v, b_v, c_v, act_v,
+    adj, xa, blk, prod, inv, w_v, b_v, c_v, act_v,
     sd, rd, sz, rz, ga, own, sb, rb, df_v,
     dwm, dwx, dwt, dwz, dwf, dwo, dbo,
     lsem, asem, zs, zr, ds, dr, xs, xr, gs, gr, fs, fr, bs, br, ws, wr,
@@ -77,6 +77,7 @@
     twin = (z, 2 * (px * SIDE + py) + other)
 
     ld_x = pltpu.make_async_copy(feat, xa.at[z], lsem.at[0])
+    ld_i = pltpu.make_async_copy(ids, adj, lsem.at[1])
     ld_w = pltpu.make_async_copy(weight, w_v, lsem.at[2])
     ld_b = pltpu.make_async_copy(bias, b_v, lsem.at[3])
     ld_c = pltpu.make_async_copy(cot, c_v, lsem.at[4])
@@ -93,6 +94,7 @@
     for off in (3, -3, 1, -1):
         pl.semaphore_signal(barrier, inc=1, device_id=at_z(off), device_id_type=MESH)
     ld_x.start()
+    ld_i.start()
 
     def greet(i, carry):
         pl.semaphore_signal(barrier, inc=1, device_id=at_chip(i), device_id_type=MESH)
@@ -107,11 +109,11 @@
     pl.semaphore_wait(barrier, 4 + 1 + CHIPS - 1)
 
     def invert(t, carry):
-        ids = [adj[s, 0, t] for s in range(SLOTS)]
+        held = [adj[s, 0, t] for s in range(SLOTS)]
         for k in range(NCOL):
             slot = jnp.int32(DEAD)
             for s in range(SLOTS):
-                slot = jnp.where(ids[s] == k, t * SLOTS + s, slot)
+                slot = jnp.where(held[s] == k, t * SLOTS + s, slot)
             inv[t, k] = slot
         return carry
 
@@ -140,6 +142,8 @@
             lax.fori_loop(0, NZ, ld_a_start, 0)
             for ld in (ld_w, ld_b, ld_c):
                 ld.start()
+        if stage == 0:
+            ld_i.wait()
         if stage < 2:
             lax.fori_loop(8 * stage, 8 * stage + 8, invert, 0)
         if stage == 1:
@@ -171,14 +175,22 @@
         remote(sz.at[i], rz.at[i], xs.at[i], xr.at[i], at_chip(i)).start()
         return carry
 
+    lag = jnp.where(core == 1, CHIPS, LAG)
+
     def to_both(i, carry):
         to_twin(i, carry)
-        return to_owner(i - LAG, carry)
-
-    lax.fori_loop(0, LAG, to_twin, 0)
-    lax.fori_loop(LAG, CHIPS, to_both, 0)
-    lax.fori_loop(CHIPS - LAG, CHIPS - 1, to_owner, 0)
+        return to_owner(i - lag, carry)
+
+    lax.fori_loop(0, lag, to_twin, 0)
+    lax.fori_loop(lag, CHIPS, to_both, 0)
+    lax.fori_loop(CHIPS - lag, CHIPS - 1, to_owner, 0)
     own[0] = both(CHIPS - 1)
+
+    def sent_x(i, carry):
+        remote(xa.at[z], xa.at[z], zs.at[i], zr.at[i], twin).wait_send()
+        return carry
+
+    lax.fori_loop(1, NZ, sent_x, 0)
 
     def collect(i, carry):
         remote(sz.at[i], rz.at[i], xs.at[i], xr.at[i], at_chip(i)).wait_recv()
@@ -203,10 +215,6 @@
     st_act.start()
     dpre = c_v[...].astype(F32) * gate * (1.0 + preact * (1.0 - gate))
     dpre_round = dpre.astype(BF16)
-    ga[c] = lax.dot_general(
-        w, dpre_round, (((1,), (1,)), ((), ())), preferred_element_type=F32
-    ).astype(BF16)
-
     tn = (((0,), (0,)), ((), ()))
     dw = lax.dot_general(agg_hi, dpre_round, tn, preferred_element_type=F32)
     dw = dw + lax.dot_general(agg_lo, dpre_round, tn, preferred_element_type=F32)
@@ -223,6 +231,10 @@
 
     lax.fori_loop(0, CHIPS - 1, w_spread, 0)
 
+    ga[c] = lax.dot_general(
+        w, dpre_round, (((1,), (1,)), ((), ())), preferred_element_type=F32
+    ).astype(BF16)
+
     def spread(i, carry):
         remote(ga.at[c], ga.at[c], gs.at[i], gr.at[i], at_chip(i)).start()
         return carry
@@ -230,6 +242,15 @@
     lax.fori_loop(0, CHIPS - 1, spread, 0)
     g_twin = remote(ga.at[c], ga.at[c], gs.at[CHIPS - 1], gr.at[CHIPS - 1], twin)
     g_twin.start()
+
+    def sent_sums(i, carry):
+        remote(sd.at[i], rd.at[i], ds.at[i], dr.at[i], twin).wait_send()
+        remote(sz.at[i], rz.at[i], xs.at[i], xr.at[i], twin).wait_send()
+        return carry
+
+    lax.fori_loop(0, CHIPS - 1, sent_sums, 0)
+    last = CHIPS - 1
+    remote(sd.at[last], rd.at[last], ds.at[last], dr.at[last], twin).wait_send()
 
     def w_collect(i, total):
         remote(dwm.at[0], dwx.at[i], wxs.at[i], wxr.at[i], at_chip(i)).wait_recv()
@@ -253,7 +274,9 @@
     dwz[z] = (jnp.where(core == 0, left, right) + dwt[1]).astype(BF16)
 
     def w_ring(i):
-        return remote(dwz.at[z], dwz.at[z], wzs.at[i], wzr.at[i], at_z(i + 1))
+        step = (i + 1) // 2
+        off = jnp.where(lax.rem(i, 2) == 0, 8 + step, 8 - step)
+        return remote(dwz.at[z], dwz.at[z], wzs.at[i], wzr.at[i], at_z(off))
 
     def w_ring_start(i, carry):
         w_ring(i).start()
@@ -303,7 +326,17 @@
         for a, b in edges:
             pull(a % NZ, 0)
     pull(0, 0)
-    for edges in REDUCE[1:]:
+
+    def sent_grads(i, carry):
+        remote(ga.at[c], ga.at[c], gs.at[i], gr.at[i], twin).wait_send()
+        remote(ga.at[c], ga.at[c], fs.at[i], fr.at[i], twin).wait_send()
+        remote(dwm.at[0], dwx.at[i], wxs.at[i], wxr.at[i], twin).wait_send()
+        return carry
+
+    lax.fori_loop(0, CHIPS - 1, sent_grads, 0)
+    g_twin.wait_send()
+    w_twin.wait_send()
+    for edges in REDUCE[1:-1]:
         for a, b in edges:
             sb[a % NZ] = summed(a).astype(BF16)
             back(a, b).start()
@@ -330,18 +363,32 @@
 
     lax.fori_loop(0, CHIPS - 1, w_gather_start, 0)
 
+    for a, b in REDUCE[-1]:
+        sb[a % NZ] = summed(a).astype(BF16)
+        back(a, b).start()
+
+    for a, b in REDUCE[0]:
+        back(a, b).wait_send()
+
+    def w_gather_wait(i, carry):
+        w_gather(i, chip(i, -1)).wait_recv()
+        return carry
+
+    lax.fori_loop(0, CHIPS - 1, w_gather_wait, 0)
+    w_back = remote(dwf.at[core], dwf.at[core], ws.at[1], wr.at[1], twin)
+    w_back.start()
+
+    def sent_pieces(i, carry):
+        w_ring(i).wait_send()
+        w_gather(i, me).wait_send()
+        return carry
+
+    lax.fori_loop(0, CHIPS - 1, sent_pieces, 0)
+
     total = summed(0)
     df_v[...] = total.T.astype(BF16)
     st_df = pltpu.make_async_copy(df_v, df_out, lsem.at[6])
     st_df.start()
-
-    def w_gather_wait(i, carry):
-        w_gather(i, chip(i, -1)).wait_recv()
-        return carry
-
-    lax.fori_loop(0, CHIPS - 1, w_gather_wait, 0)
-    w_back = remote(dwf.at[core], dwf.at[core], ws.at[1], wr.at[1], twin)
-    w_back.start()
 
     w_in = remote(dwf.at[other], dwf.at[other], ws.at[1], wr.at[1], twin)
     w_in.wait_recv()
@@ -354,25 +401,9 @@
     st_db = pltpu.make_async_copy(dbo, db_out, lsem.at[8])
     st_db.start()
 
-    def drain(i, carry):
-        remote(sd.at[i], rd.at[i], ds.at[i], dr.at[i], twin).wait_send()
-        remote(ga.at[c], ga.at[c], gs.at[i], gr.at[i], twin).wait_send()
-        return carry
-
-    lax.fori_loop(0, CHIPS, drain, 0)
-
-    def drain_15(i, carry):
-        remote(sz.at[i], rz.at[i], xs.at[i], xr.at[i], twin).wait_send()
-        remote(ga.at[c], ga.at[c], fs.at[i], fr.at[i], twin).wait_send()
-        remote(dwm.at[0], dwx.at[i], wxs.at[i], wxr.at[i], twin).wait_send()
-        remote(dwz.at[z], dwz.at[z], wzs.at[i], wzr.at[i], twin).wait_send()
-        w_gather(i, me).wait_send()
-        remote(xa.at[z], xa.at[z], zs.at[i + 1], zr.at[i + 1], twin).wait_send()
-        remote(sb.at[i], rb.at[i], bs.at[i + 1], br.at[i + 1], twin).wait_send()
-        return carry
-
-    lax.fori_loop(0, CHIPS - 1, drain_15, 0)
-    w_twin.wait_send()
+    for edges in REDUCE[1:]:
+        for a, b in edges:
+            back(a, b).wait_send()
     w_back.wait_send()
     for st in (st_act, st_df, st_dw, st_db):
         st.wait()
@@ -401,9 +432,10 @@
             jax.ShapeDtypeStruct((F_IN, F_OUT), F32),
             jax.ShapeDtypeStruct((1, F_OUT), F32),
         ),
-        in_specs=[pl.BlockSpec(memory_space=pltpu.SMEM)] + [any_space] * 5,
+        in_specs=[any_space] * 6,
         out_specs=[any_space] * 4,
         scratch_shapes=[
+            pltpu.SMEM((SLOTS, 1, NZ), jnp.int32),
             pltpu.VMEM((NZ, BLOCK, F_IN), BF16),
             pltpu.VMEM((DEAD, BLOCK, BLOCK), BF16),
             pltpu.VMEM((DEAD + 1, BLOCK, F_IN), F32),

time: 77.2 us -> 73 us (0.946)
  Pallas kernels: 76.4 us -> 72.1 us
    pallas_call x1, Pallas kernels: 74.7 us -> 70.5 us  [local(): pl.pallas_call(kernel, out_shape=(jax.ShapeDtypeStruct((BLOCK, F_OUT), BF...]
where the time goes in v3:
time: 73 us; the launch traced here: 72.8 us
  Pallas kernels  72.1 us (99%)
    pallas_call x1, Pallas kernels, local(): pl.pallas_call(kernel, out_shape=(jax.ShapeDtypeStruct((BLOCK, F_OUT), BF...  70.5 us
    pallas_call x1, Pallas kernels, local(): pl.pallas_call(hand_over, out_shape=tuple((jax.ShapeDtypeStruct(o.shape,...  1.69 us

profile of v3, /device:TPU:1, one launch (start us, length us, event | category | flops | bytes accessed | tf_op | source)
XLA Modules:
  0.0 72.8 jit_solution(18159922355736334113)
XLA Ops:
  0.6 70.5 %shard_map.93 = (bf16[128,256]{1,0:T(8,128)(2,1)}, bf16[128,128]{1,0:T(8,128)(2,1)}, f32[128,256]{1,0:T(8,128)}, f32[1,256]{1,0:T(1,128)}) custom-call(s32[6,1,16]{2,1,0:T(1,128)} %bitcast.5, bf16[128,128]{1,0:T(8,128)(2,1)} %feat.1, bf16[128,256]{1,0:T(8,128)(2,1)} %weight.1, f32[1,256]{1,0:T(1,128)} %bitcast.6, bf16[96,128,128]{2,1,0:T(8,128)(2,1)} %bitcast.4, ...), custom_call_target="tpu_custom_call" | custom-call | tf_op jit(solution)/shard_map/pallas_call | solution.py:427
  71.1 1.7 %shard_map.94 = (bf16[128,256]{1,0:T(8,128)(2,1)}, bf16[128,128]{1,0:T(8,128)(2,1)}, f32[128,256]{1,0:T(8,128)}, f32[1,256]{1,0:T(1,128)}) custom-call(bf16[128,256]{1,0:T(8,128)(2,1)} %get-tuple-element.12.refs_0_, bf16[128,128]{1,0:T(8,128)(2,1)} %get-tuple-element.13.refs_1_, f32[128,256]{1,0:T(8,128)} %get-tuple-element.14.refs_2_, ...), custom_call_target="tpu_custom_call" | custom-call | tf_op jit(solution)/shard_map/pallas_call | solution.py:487

commit v4 on v3

--- a/solution.py
+++ b/solution.py
@@ -18,6 +18,7 @@
 NCOL = 2 * CHIPS
 DEAD = NZ * SLOTS
 LAG = 2
+EARLY = (4, 8, 12, 16)
 HALFWAY = 0
 GATHER = (
     ((0, 3), (0, -3), (0, 1), (0, -1)),
@@ -25,8 +26,8 @@
     ((6, 8), (6, 7), (-6, -7), (6, 5), (-6, -5)),
 )
 REDUCE = (
-    ((8, 6), (7, 6), (-7, -6), (5, 6), (-5, -6), (4, 3), (-4, -3), (1, 0), (-1, 0)),
-    ((6, 3), (-6, -3), (2, 0), (-2, 0)),
+    ((8, 6), (7, 6), (-7, -6), (5, 6), (-5, -6), (4, 3), (-4, -3), (1, 0), (-1, 0), (2, 0), (-2, 0)),
+    ((6, 3), (-6, -3)),
     ((3, 0), (-3, 0)),
 )
 
@@ -105,8 +106,9 @@
 
     prod[DEAD] = jnp.zeros((BLOCK, F_IN), F32)
     ga[NCOL] = jnp.zeros((F_IN, BLOCK), BF16)
-    ld_x.wait()
-    pl.semaphore_wait(barrier, 4 + 1 + CHIPS - 1)
+    lax.fori_loop(0, NZ, ld_a_start, 0)
+    for ld in (ld_w, ld_b, ld_c):
+        ld.start()
 
     def invert(t, carry):
         held = [adj[s, 0, t] for s in range(SLOTS)]
@@ -117,6 +119,12 @@
             inv[t, k] = slot
         return carry
 
+    ld_i.wait()
+    lax.fori_loop(0, EARLY[0], invert, 0)
+    ld_x.wait()
+    pl.semaphore_wait(barrier, 4 + 1 + CHIPS - 1)
+
+
     def multiply(t):
         ld_a(t).wait()
         tall = blk[pl.ds(t * SLOTS, SLOTS)].reshape(SLOTS * BLOCK, BLOCK)
@@ -138,14 +146,7 @@
         for a, b in edges:
             arrive(a)
             hop(a, b).start()
-        if stage == 0:
-            lax.fori_loop(0, NZ, ld_a_start, 0)
-            for ld in (ld_w, ld_b, ld_c):
-                ld.start()
-        if stage == 0:
-            ld_i.wait()
-        if stage < 2:
-            lax.fori_loop(8 * stage, 8 * stage + 8, invert, 0)
+        lax.fori_loop(EARLY[stage], EARLY[stage + 1], invert, 0)
         if stage == 1:
             for b in (0, 1, -1, 3, -3):
                 multiply(ring(-b))

time: 73 us -> 72.9 us (level)
  no operation moved by 1% of the time
where the time goes in v4:
time: 72.9 us; the launch traced here: 72.4 us
  Pallas kernels  71.8 us (98%)
    pallas_call x1, Pallas kernels, local(): pl.pallas_call(kernel, out_shape=(jax.ShapeDtypeStruct((BLOCK, F_OUT), BF...  70.1 us
    pallas_call x1, Pallas kernels, local(): pl.pallas_call(hand_over, out_shape=tuple((jax.ShapeDtypeStruct(o.shape,...  1.69 us

profile of v4, /device:TPU:1, one launch (start us, length us, event | category | flops | bytes accessed | tf_op | source)
XLA Modules:
  0.0 72.4 jit_solution(1799125795210280176)
XLA Ops:
  0.6 70.1 %shard_map.93 = (bf16[128,256]{1,0:T(8,128)(2,1)}, bf16[128,128]{1,0:T(8,128)(2,1)}, f32[128,256]{1,0:T(8,128)}, f32[1,256]{1,0:T(1,128)}) custom-call(s32[6,1,16]{2,1,0:T(1,128)} %bitcast.5, bf16[128,128]{1,0:T(8,128)(2,1)} %feat.1, bf16[128,256]{1,0:T(8,128)(2,1)} %weight.1, f32[1,256]{1,0:T(1,128)} %bitcast.6, bf16[96,128,128]{2,1,0:T(8,128)(2,1)} %bitcast.4, ...), custom_call_target="tpu_custom_call" | custom-call | tf_op jit(solution)/shard_map/pallas_call | solution.py:428
  70.7 1.7 %shard_map.94 = (bf16[128,256]{1,0:T(8,128)(2,1)}, bf16[128,128]{1,0:T(8,128)(2,1)}, f32[128,256]{1,0:T(8,128)}, f32[1,256]{1,0:T(1,128)}) custom-call(bf16[128,256]{1,0:T(8,128)(2,1)} %get-tuple-element.12.refs_0_, bf16[128,128]{1,0:T(8,128)(2,1)} %get-tuple-element.13.refs_1_, f32[128,256]{1,0:T(8,128)} %get-tuple-element.14.refs_2_, ...), custom_call_target="tpu_custom_call" | custom-call | tf_op jit(solution)/shard_map/pallas_call | solution.py:488
